TPU v7x, 32 devices: a whole 2x2x4 slice. The times are simulated.
32 devices in a mesh: section: 4 (over x, core), row: 8 (over z, y).
Axes of the slice: x: 2, y: 2, z: 4, core: 2. Of those that a mesh axis runs over, the one named last changes fastest.
Arguments:
- pair_in: bfloat16 [4, 256, 256, 128], P('section', 'row'), may hold values from -6 to 6
- upstream: bfloat16 [4, 256, 256, 128], P('section', 'row'), may hold values from -6 to 6
- chain_ids: int32 [256], replicated, may hold values from 0 to 2, never falling along the last dimension, each value on 1 to 192 neighbouring positions
- crop_mask: int32 [256], replicated, may hold values 0 or 1
- weight_in: bfloat16 [4, 2, 128, 640], P('section'), may hold values from -0.5 to 0.5
- weight_out: bfloat16 [4, 2, 128, 128], P('section'), may hold values from -0.5 to 0.5
- gain_in: float32 [4, 2, 128], P('section'), may hold values from 0.25 to 1.75
- bias_in: float32 [4, 2, 128], P('section'), may hold values from -3 to 3
- gain_out: float32 [4, 2, 128], P('section'), may hold values from 0.25 to 1.75
- bias_out: float32 [4, 2, 128], P('section'), may hold values from -3 to 3
Outputs:
- next_cotangent: bfloat16 [4, 256, 256, 128], P('section', 'row')
- grad_weight_in: float32 [4, 2, 128, 640], P('section')
- grad_weight_out: float32 [4, 2, 128, 128], P('section')
- grad_norm_in: float32 [4, 2, 2, 128], P('section')
- grad_norm_out: float32 [4, 2, 2, 128], P('section')
Inputs may be any that keep to these rules, and one draw needn't show every extreme that they name: `chain_ids`: chain numbers never fall along the residues; the longest chain holds 192 residues. `crop_mask`: 1 marks a residue present in the crop.
All inputs are finite; a program needn't handle non-finite values.
Results may differ from a plain program's by a relative error of at most 0.014.
Values may be sent and summed in bfloat16 or wider, within the bound.
A program may use at most 192 MiB of HBM per device.

v0:
```python
import jax
import jax.numpy as jnp
from jax import lax
from jax.sharding import PartitionSpec as P

epsilon = 1e-05


def passed_along(array, axis, by):
    length = lax.axis_size(axis)
    return lax.ppermute(array, axis, [(i, (i + by) % length) for i in range(length)])


def multiply(pattern, first_part, second):
    return jnp.einsum(pattern, first_part, second, preferred_element_type=jnp.float32)


def fold(array):
    quarter = array.shape[-1] // 4
    half = array.shape[0] // 2
    tail = array[..., 2 * quarter : 3 * quarter]
    zeros = jnp.zeros_like(tail)
    kept = array[..., : 2 * quarter] + jnp.concatenate([array[..., 3 * quarter :], zeros], axis=-1)
    return jnp.concatenate([kept[:half], kept[half:], tail[:half], tail[half:]], axis=-1)


def unfold(array, mask):
    quarter = array.shape[-1] // 6

    def one(kept, tail):
        return jnp.concatenate([kept, tail, kept[..., :quarter]], axis=-1)

    both = jnp.concatenate(
        [
            one(array[..., : 2 * quarter], array[..., 4 * quarter : 5 * quarter]),
            one(array[..., 2 * quarter : 4 * quarter], array[..., 5 * quarter :]),
        ],
        axis=0,
    )
    if mask is None:
        return both
    return jnp.where(mask, both, jnp.zeros_like(both))


def to_channels(array, mask):
    moved = lax.all_to_all(fold(array), "row", split_axis=0, concat_axis=1, tiled=True)
    return unfold(moved, mask)


def to_rows(array, mask):
    moved = lax.all_to_all(fold(array), "row", split_axis=1, concat_axis=0, tiled=True)
    return unfold(moved, mask)


def reduced(sums):
    weights_in, weights_out, norm_in, norm_out = sums
    norms = jnp.concatenate([norm_in, norm_out], axis=0)
    columns = weights_out.shape[1]
    norms = jnp.pad(norms, ((0, columns - norms.shape[0]), (0, 0))).T
    flat = jnp.concatenate([weights_in, weights_out, norms], axis=1).astype(jnp.bfloat16)
    width = lax.axis_size("row")
    parts = flat.reshape(width, flat.shape[0] // width, flat.shape[1])
    parts = lax.all_to_all(parts, "row", split_axis=0, concat_axis=0, tiled=True)
    summed = jnp.sum(parts.astype(jnp.float32), axis=0).astype(jnp.bfloat16)
    total = lax.all_gather(summed, "row", axis=0, tiled=True).astype(jnp.float32)
    split = weights_in.shape[1]
    norms = total[:, split + columns : split + columns + 4].T
    return (total[:, :split], total[:, split : split + columns], norms[:2], norms[2:])


def layer_inputs(pair_rows, pair_mask, weight_inner, gain_inner, bias_inner, hidden):
    values = pair_rows.astype(jnp.float32)
    centered = values - jnp.mean(values, axis=-1, keepdims=True)
    inverse_scale = lax.rsqrt(jnp.mean(centered * centered, axis=-1, keepdims=True) + epsilon)
    normal_in = centered * inverse_scale
    normed = (normal_in * gain_inner + bias_inner).astype(jnp.bfloat16)
    projected = multiply("rnc,cf->frn", normed, weight_inner[:, : 4 * hidden])
    gating = jax.nn.sigmoid(multiply("rnc,cf->rnf", normed, weight_inner[:, 4 * hidden :]))
    left_sigmoid = jax.nn.sigmoid(projected[:hidden])
    right_sigmoid = jax.nn.sigmoid(projected[2 * hidden : 3 * hidden])
    left_edges = (pair_mask * left_sigmoid * projected[hidden : 2 * hidden]).astype(jnp.bfloat16)
    right_edges = (pair_mask * right_sigmoid * projected[3 * hidden :]).astype(jnp.bfloat16)
    saved_in = (normal_in, inverse_scale, normed, projected, left_sigmoid, right_sigmoid, gating)
    return (left_edges, right_edges, saved_in)


def triangle_forward(left_edges, right_edges, outgoing):
    if outgoing:
        product = multiply("hik,hjk->hij", left_edges, right_edges)
    else:
        product = multiply("hki,hkj->hij", left_edges, right_edges)
    return product.astype(jnp.bfloat16)


def triangle_backward(grad_product, left_edges, right_edges, outgoing):
    if outgoing:
        grad_leftside = multiply("hij,hjk->hik", grad_product, right_edges)
        grad_rightside = multiply("hij,hik->hjk", grad_product, left_edges)
    else:
        grad_leftside = multiply("hij,hkj->hki", grad_product, right_edges)
        grad_rightside = multiply("hij,hki->hkj", grad_product, left_edges)
    return (grad_leftside.astype(jnp.bfloat16), grad_rightside.astype(jnp.bfloat16))


def layer_output(pair_rows, product, gating, gain_outer, bias_outer, weight_outer):
    values = product.astype(jnp.float32)
    centered = values - jnp.mean(values, axis=0, keepdims=True)
    inverse_scale = lax.rsqrt(jnp.mean(centered * centered, axis=0, keepdims=True) + epsilon)
    normal_out = centered * inverse_scale
    normed = (normal_out * gain_outer[:, None, None] + bias_outer[:, None, None]).astype(
        jnp.bfloat16
    )
    branch = multiply("hrn,hc->rnc", normed, weight_outer)
    updated = (pair_rows.astype(jnp.float32) + gating * branch).astype(jnp.bfloat16)
    return (updated, (normal_out, inverse_scale, normed, branch))


def output_backward(grad_pair, gating, saved_out, gain_outer, weight_outer):
    normal_out, inverse_scale, normed, branch = saved_out
    upstream_values = grad_pair.astype(jnp.float32)
    grad_branch = (upstream_values * gating).astype(jnp.bfloat16)
    grad_gate = (upstream_values * branch * gating * (1.0 - gating)).astype(jnp.bfloat16)
    grad_weight_out = multiply("hrn,rnc->hc", normed, grad_branch)
    grad_normed = multiply("rnc,hc->hrn", grad_branch, weight_outer)
    grad_gain = jnp.sum(grad_normed * normal_out, axis=(1, 2))
    grad_bias = jnp.sum(grad_normed, axis=(1, 2))
    scaled = grad_normed * gain_outer[:, None, None]
    grad_product = inverse_scale * (
        scaled
        - jnp.mean(scaled, axis=0, keepdims=True)
        - normal_out * jnp.mean(scaled * normal_out, axis=0, keepdims=True)
    )
    return (
        grad_product.astype(jnp.bfloat16),
        grad_gate,
        grad_weight_out,
        jnp.stack([grad_gain, grad_bias]),
    )


def input_backward(
    grad_leftside, grad_rightside, grad_gate, saved_in, pair_mask, weight_inner, gain_inner, hidden
):
    normal_in, inverse_scale, normed, projected, left_sigmoid, right_sigmoid, gating = saved_in
    left_values = grad_leftside.astype(jnp.float32) * pair_mask
    right_values = grad_rightside.astype(jnp.float32) * pair_mask
    grad_projected = jnp.concatenate(
        [
            left_values * projected[hidden : 2 * hidden] * left_sigmoid * (1.0 - left_sigmoid),
            left_values * left_sigmoid,
            right_values * projected[3 * hidden :] * right_sigmoid * (1.0 - right_sigmoid),
            right_values * right_sigmoid,
        ],
        axis=0,
    ).astype(jnp.bfloat16)
    grad_weight_in = jnp.concatenate(
        [
            multiply("rnc,frn->cf", normed, grad_projected),
            multiply("rnc,rnf->cf", normed, grad_gate),
        ],
        axis=1,
    )
    grad_normed = multiply("frn,cf->rnc", grad_projected, weight_inner[:, : 4 * hidden]) + multiply(
        "rnf,cf->rnc", grad_gate, weight_inner[:, 4 * hidden :]
    )
    grad_gain = jnp.sum(grad_normed * normal_in, axis=(0, 1))
    grad_bias = jnp.sum(grad_normed, axis=(0, 1))
    scaled = grad_normed * gain_inner
    grad_pair = inverse_scale * (
        scaled
        - jnp.mean(scaled, axis=-1, keepdims=True)
        - normal_in * jnp.mean(scaled * normal_in, axis=-1, keepdims=True)
    )
    return (grad_pair, grad_weight_in, jnp.stack([grad_gain, grad_bias]))


def per_device(
    pair_in,
    upstream,
    chain_ids,
    crop_mask,
    weight_in,
    weight_out,
    gain_in,
    bias_in,
    gain_out,
    bias_out,
):
    row_count = pair_in.shape[1]
    hidden = weight_out.shape[2]
    row_start = lax.axis_index("row") * row_count
    row_chain = lax.dynamic_slice_in_dim(chain_ids, row_start, row_count)
    row_crop = lax.dynamic_slice_in_dim(crop_mask, row_start, row_count)
    same_chain = row_chain[:, None] == chain_ids[None, :]
    pair_mask = jnp.where(same_chain, row_crop[:, None] * crop_mask[None, :], 0).astype(jnp.float32)
    row_mask = pair_mask > 0
    full_mask = (chain_ids[:, None] == chain_ids[None, :]) & (
        crop_mask[:, None] * crop_mask[None, :] > 0
    )
    pair_rows = pair_in[0]
    grad_top = upstream[0]

    def forward_update(source, direction, outgoing):
        left_edges, right_edges, saved_in = layer_inputs(
            source,
            pair_mask,
            weight_in[0, direction],
            gain_in[0, direction],
            bias_in[0, direction],
            hidden,
        )
        left_channels = to_channels(left_edges, full_mask)
        right_channels = to_channels(right_edges, full_mask)
        product = to_rows(triangle_forward(left_channels, right_channels, outgoing), row_mask)
        updated, saved_out = layer_output(
            source,
            product,
            saved_in[6],
            gain_out[0, direction],
            bias_out[0, direction],
            weight_out[0, direction],
        )
        return (updated, (left_channels, right_channels, saved_in, saved_out))

    def backward_update(grad_pair, stored, direction, outgoing):
        left_channels, right_channels, saved_in, saved_out = stored
        grad_product, grad_gate, grad_weight_out, grad_norm_out = output_backward(
            grad_pair, saved_in[6], saved_out, gain_out[0, direction], weight_out[0, direction]
        )
        grad_product = jnp.where(row_mask, grad_product, jnp.zeros_like(grad_product))
        grad_channels = to_channels(grad_product, full_mask)
        left_grads, right_grads = triangle_backward(
            grad_channels, left_channels, right_channels, outgoing
        )
        left_grads = jnp.where(full_mask, left_grads, jnp.zeros_like(left_grads))
        right_grads = jnp.where(full_mask, right_grads, jnp.zeros_like(right_grads))
        grad_leftside = to_rows(left_grads, None)
        grad_rightside = to_rows(right_grads, None)
        branch_grad, grad_weight_in, grad_norm_in = input_backward(
            grad_leftside,
            grad_rightside,
            grad_gate,
            saved_in,
            pair_mask,
            weight_in[0, direction],
            gain_in[0, direction],
            hidden,
        )
        return (branch_grad, (grad_weight_in, grad_weight_out, grad_norm_in, grad_norm_out))

    middle, stored_outgoing = forward_update(pair_rows, 0, True)
    top_unused, stored_incoming = forward_update(middle, 1, False)
    grad_inner, sums_incoming = backward_update(grad_top, stored_incoming, 1, False)
    grad_middle = (grad_top.astype(jnp.float32) + grad_inner).astype(jnp.bfloat16)
    grad_outer, sums_outgoing = backward_update(grad_middle, stored_outgoing, 0, True)
    outer_rounded = lax.optimization_barrier(grad_outer.astype(jnp.bfloat16))
    grad_input = (grad_middle.astype(jnp.float32) + outer_rounded.astype(jnp.float32)).astype(
        jnp.bfloat16
    )
    passed_back = passed_along(grad_input, "section", -1)
    incoming_totals = reduced(sums_incoming)
    outgoing_totals = reduced(sums_outgoing)
    totals = [jnp.stack([outgoing_totals[member], incoming_totals[member]]) for member in range(4)]
    inverse_n = 1.0 / pair_rows.shape[1]
    return (
        passed_back[None],
        totals[0][None] * inverse_n,
        totals[1][None] * inverse_n,
        totals[2][None] * inverse_n,
        totals[3][None] * inverse_n,
    )


def solution(mesh):
    return jax.shard_map(
        per_device,
        mesh=mesh,
        in_specs=(
            P("section", "row", None, None),
            P("section", "row", None, None),
            P(),
            P(),
            P("section", None, None, None),
            P("section", None, None, None),
            P("section", None, None),
            P("section", None, None),
            P("section", None, None),
            P("section", None, None),
        ),
        out_specs=(
            P("section", "row", None, None),
            P("section", None, None, None),
            P("section", None, None, None),
            P("section", None, None, None),
            P("section", None, None, None),
        ),
        check_vma=False,
    )
```

profile of v0, /device:TPU:0, one launch (start us, length us, event | category | flops | bytes accessed | tf_op | source)
XLA Modules:
  0.0 846.4 jit_solution(3344272591239111677)
XLA Ops:
  3.4 3.3 copy.460
  10.5 5.1 multiply_convert_fusion.11
  20.1 4.8 copy.473
  25.0 7.3 all-to-all-start.1
  38.8 4.8 copy.465
  43.7 25.7 %all-to-all-done.1 = bf16[64,32,384]{2,1,0:T(8,128)(2,1)} async-done(((bf16[64,32,384]{2,1,0:T(8,128)(2,1)}), bf16[64,32,384]{2,1,0:T(8,128)(2,1)}, u32[]{:S(2)}, u32[]{:S(2)}) %all-to-all-start.1) | async-done | bytes 1572896 | tf_op jit(solution)/shard_map/all_to_all | solution.py:46
  69.3 4.6 all-to-all-start
  77.7 32.8 %all-to-all-done = bf16[64,32,384]{2,1,0:T(8,128)(2,1)} async-done(((bf16[64,32,384]{2,1,0:T(8,128)(2,1)}), bf16[64,32,384]{2,1,0:T(8,128)(2,1)}, u32[]{:S(2)}, u32[]{:S(2)}) %all-to-all-start) | async-done | bytes 1572896 | tf_op jit(solution)/shard_map/all_to_all | solution.py:46
  141.1 4.8 all-to-all-start.2
  146.6 36.0 %all-to-all-done.2 = bf16[8,256,384]{2,0,1:T(8,128)(2,1)} async-done(((bf16[8,256,384]{2,0,1:T(8,128)(2,1)}), bf16[8,256,384]{2,0,1:T(8,128)(2,1)}, u32[]{:S(2)}, u32[]{:S(2)}) %all-to-all-start.2) | async-done | bytes 1572896 | tf_op jit(solution)/shard_map/all_to_all | solution.py:51
  189.3 4.6 convert_reduce_fusion.1
  197.7 5.0 multiply_convert_fusion.9
  206.0 3.3 copy.496
  209.3 4.6 all-to-all-start.4
  216.8 3.2 copy.488
  219.9 30.6 %all-to-all-done.4 = bf16[64,32,384]{2,1,0:T(8,128)(2,1)} async-done(((bf16[64,32,384]{2,1,0:T(8,128)(2,1)}), bf16[64,32,384]{2,1,0:T(8,128)(2,1)}, u32[]{:S(2)}, u32[]{:S(2)}) %all-to-all-start.4) | async-done | bytes 1572896 | tf_op jit(solution)/shard_map/all_to_all | solution.py:46
  250.5 3.6 all-to-all-start.3
  257.7 33.7 %all-to-all-done.3 = bf16[64,32,384]{2,1,0:T(8,128)(2,1)S(1)} async-done(((bf16[64,32,384]{2,1,0:T(8,128)(2,1)}), bf16[64,32,384]{2,1,0:T(8,128)(2,1)S(1)}, u32[]{:S(2)}, u32[]{:S(2)}) %all-to-all-start.3) | async-done | bytes 1572896 | tf_op jit(solution)/shard_map/all_to_all | solution.py:46
  310.6 4.8 all-to-all-start.5
  315.5 4.1 copy.459
  319.6 3.8 add_divide_fusion
  323.4 28.7 %all-to-all-done.5 = bf16[8,256,384]{2,0,1:T(8,128)(2,1)} async-done(((bf16[8,256,384]{2,0,1:T(8,128)(2,1)}), bf16[8,256,384]{2,0,1:T(8,128)(2,1)}, u32[]{:S(2)}, u32[]{:S(2)}) %all-to-all-start.5) | async-done | bytes 1572896 | tf_op jit(solution)/shard_map/all_to_all | solution.py:51
  364.8 40.7 %all_to_all.226 = bf16[64,32,384]{2,1,0:T(8,128)(2,1)S(1)} all-to-all(bf16[64,32,384]{2,1,0:T(8,128)(2,1)S(1)} %copy.511), channel_id=1, replica_groups=mesh['section'=4,'row'=8] {'row'}, dimensions={0} | all-to-all | bytes 3145728 | tf_op jit(solution)/shard_map/all_to_all | solution.py:46
  423.7 4.3 all-to-all-start.8
  435.5 28.7 %all-to-all-done.8 = bf16[8,256,384]{2,0,1:T(8,128)(2,1)} async-done(((bf16[8,256,384]{2,0,1:T(8,128)(2,1)}), bf16[8,256,384]{2,0,1:T(8,128)(2,1)}, u32[]{:S(2)}, u32[]{:S(2)}) %all-to-all-start.8) | async-done | bytes 1572896 | tf_op jit(solution)/shard_map/all_to_all | solution.py:51
  464.2 4.3 all-to-all-start.7
  468.5 6.0 fusion.68
  479.0 26.0 %all-to-all-done.7 = bf16[8,256,384]{2,0,1:T(8,128)(2,1)} async-done(((bf16[8,256,384]{2,0,1:T(8,128)(2,1)}), bf16[8,256,384]{2,0,1:T(8,128)(2,1)}, u32[]{:S(2)}, u32[]{:S(2)}) %all-to-all-start.7) | async-done | bytes 1572896 | tf_op jit(solution)/shard_map/all_to_all | solution.py:51
  538.0 6.6 multiply_convert_fusion.5
  544.7 7.6 multiply_convert_fusion.7
  561.3 4.2 fusion.63
  574.2 4.6 all-to-all-start.9
  581.3 3.3 fusion.103
  586.9 4.8 fusion.98
  592.4 23.0 %all-to-all-done.9 = bf16[64,32,384]{2,1,0:T(8,128)(2,1)} async-done(((bf16[64,32,384]{2,1,0:T(8,128)(2,1)}), bf16[64,32,384]{2,1,0:T(8,128)(2,1)}, u32[]{:S(2)}, u32[]{:S(2)}) %all-to-all-start.9) | async-done | bytes 1572896 | tf_op jit(solution)/shard_map/all_to_all | solution.py:46
  615.4 3.6 all-to-all-start.13
  629.5 6.0 all-to-all-start.11
  642.6 29.7 %all-to-all-done.11 = bf16[8,256,384]{2,0,1:T(8,128)(2,1)} async-done(((bf16[8,256,384]{2,0,1:T(8,128)(2,1)}), bf16[8,256,384]{2,0,1:T(8,128)(2,1)}, u32[]{:S(2)}, u32[]{:S(2)}) %all-to-all-start.11) | async-done | bytes 1572896 | tf_op jit(solution)/shard_map/all_to_all | solution.py:51
  672.3 4.5 all-to-all-start.10
  681.7 3.7 fusion.105
  685.4 4.1 fusion.102
  689.5 44.1 %all_gather.7 = bf16[128,896]{1,0:T(8,128)(2,1)S(1)} all-gather(bf16[16,896]{1,0:T(8,128)(2,1)S(1)} %reduce_sum.265), channel_id=1, replica_groups=mesh['section'=4,'row'=8] {'row'}, dimensions={0}, use_global_device_ids=true | all-gather | bytes 258048 | tf_op jit(solution)/shard_map/all_gather | solution.py:65
  772.4 6.7 multiply_convert_fusion.1
  779.2 5.8 multiply_convert_fusion.3
  795.1 3.8 all-to-all-start.12
  799.0 9.0 %all-to-all-done.12 = bf16[8,16,896]{2,1,0:T(8,128)(2,1)S(1)} async-done(((bf16[8,16,896]{2,1,0:T(8,128)(2,1)}), bf16[8,16,896]{2,1,0:T(8,128)(2,1)S(1)}, u32[]{:S(2)}, u32[]{:S(2)}) %all-to-all-start.12) | async-done | bytes 229408 | tf_op jit(solution)/shard_map/all_to_all | solution.py:63
  808.0 30.8 %all_gather.6 = bf16[128,896]{1,0:T(8,128)(2,1)S(1)} all-gather(bf16[16,896]{1,0:T(8,128)(2,1)S(1)} %reduce_sum.260), channel_id=1, replica_groups=mesh['section'=4,'row'=8] {'row'}, dimensions={0}, use_global_device_ids=true | all-gather | bytes 258048 | tf_op jit(solution)/shard_map/all_gather | solution.py:65
  841.9 4.1 copy.592
  (476 shorter events, 263.4 us)
Async XLA Ops:
  6.7 182.4 %copy-start.2 = (bf16[1,32,256,128]{2,3,1,0:T(8,128)(2,1)}, bf16[1,32,256,128]{2,3,1,0:T(8,128)(2,1)S(1)}, u32[]{:S(2)}) copy-start(bf16[1,32,256,128]{2,3,1,0:T(8,128)(2,1)S(1)} %copy.460) | copy-start | bytes 6291460
  7.1 182.1 %copy-start.50 = (f32[32,256]{1,0:T(8,128)}, f32[32,256]{1,0:T(8,128)S(1)}, u32[]{:S(2)}) copy-start(f32[32,256]{1,0:T(8,128)S(1)} %broadcast_multiply_fusion.11) | copy-start | bytes 98308
  7.9 181.3 %copy-start.54 = (f32[32,256]{1,0:T(8,128)}, f32[32,256]{1,0:T(8,128)S(1)}, u32[]{:S(2)}) copy-start(f32[32,256]{1,0:T(8,128)S(1)} %add_rsqrt_fusion.3) | copy-start | bytes 98308
  7.9 181.3 %copy-start.91 = (f32[128]{0:T(128)}, f32[128]{0:T(128)S(1)}, u32[]{:S(2)}) copy-start(f32[128]{0:T(128)S(1)} %get-tuple-element.203) | copy-start | bytes 1540
  7.9 181.3 %copy-start.97 = (f32[128]{0:T(128)}, f32[128]{0:T(128)S(1)}, u32[]{:S(2)}) copy-start(f32[128]{0:T(128)S(1)} %get-tuple-element.197) | copy-start | bytes 1540
  7.9 311.6 %copy-start.101 = (f32[128]{0:T(128)}, f32[128]{0:T(128)S(1)}, u32[]{:S(2)}) copy-start(f32[128]{0:T(128)S(1)} %get-tuple-element.196) | copy-start | bytes 1540
  25.0 44.4 %all-to-all-start.1 = ((bf16[64,32,384]{2,1,0:T(8,128)(2,1)}), bf16[64,32,384]{2,1,0:T(8,128)(2,1)}, u32[]{:S(2)}, u32[]{:S(2)}) async-start(bf16[64,32,384]{2,1,0:T(8,128)(2,1)} %copy.473), calls=%async_computation.1 | async-start | bytes 3145728 | tf_op jit(solution)/shard_map/all_to_all | solution.py:46
  69.3 41.2 %all-to-all-start = ((bf16[64,32,384]{2,1,0:T(8,128)(2,1)}), bf16[64,32,384]{2,1,0:T(8,128)(2,1)}, u32[]{:S(2)}, u32[]{:S(2)}) async-start(bf16[64,32,384]{2,1,0:T(8,128)(2,1)} %copy.465), calls=%async_computation | async-start | bytes 3145728 | tf_op jit(solution)/shard_map/all_to_all | solution.py:46
  74.1 59.5 %copy-start.87 = (pred[256,256]{0,1:T(8,128)(4,1)}, pred[256,256]{0,1:T(8,128)(4,1)S(1)}, u32[]{:S(2)}) copy-start(pred[256,256]{0,1:T(8,128)(4,1)S(1)} %fusion.108) | copy-start | bytes 196612
  116.2 10.9 %copy-start.39 = (bf16[8,256,128]{2,1,0:T(8,128)(2,1)S(1)}, bf16[8,256,128]{2,1,0:T(8,128)(2,1)}, u32[]{:S(2)}) copy-start(bf16[8,256,128]{2,1,0:T(8,128)(2,1)} %get-tuple-element.149) | copy-start | bytes 1572868
  117.3 15.4 %copy-start.41 = (bf16[8,256,64]{2,1,0:T(8,128)(2,1)S(1)}, bf16[8,256,64]{2,1,0:T(8,128)(2,1)}, u32[]{:S(2)}) copy-start(bf16[8,256,64]{2,1,0:T(8,128)(2,1)} %get-tuple-element.153) | copy-start | bytes 786436
  136.9 9.0 %copy-start.111 = (f32[1,2,128]{2,1,0:T(2,128)S(1)}, f32[1,2,128]{2,1,0:T(2,128)}, u32[]{:S(2)}) copy-start(f32[1,2,128]{2,1,0:T(2,128)} %param.19) | copy-start | bytes 3076
  136.9 9.0 %copy-start.112 = (f32[1,2,128]{2,1,0:T(2,128)S(1)}, f32[1,2,128]{2,1,0:T(2,128)}, u32[]{:S(2)}) copy-start(f32[1,2,128]{2,1,0:T(2,128)} %param.18) | copy-start | bytes 3076
  136.9 9.5 %copy-start.106 = (s32[32]{0:T(128)S(1)}, s32[32]{0:T(128)}, u32[]{:S(2)}) copy-start(s32[32]{0:T(128)} %copy-done.105) | copy-start | bytes 388
  141.1 41.4 %all-to-all-start.2 = ((bf16[8,256,384]{2,0,1:T(8,128)(2,1)}), bf16[8,256,384]{2,0,1:T(8,128)(2,1)}, u32[]{:S(2)}, u32[]{:S(2)}) async-start(bf16[8,256,384]{2,0,1:T(8,128)(2,1)} %copy.483), calls=%async_computation.2 | async-start | bytes 3145728 | tf_op jit(solution)/shard_map/all_to_all | solution.py:51
  146.5 41.1 %copy-start.93 = (f32[128]{0:T(128)}, f32[128]{0:T(128)S(1)}, u32[]{:S(2)}) copy-start(f32[128]{0:T(128)S(1)} %get-tuple-element.205) | copy-start | bytes 1540
  146.5 41.1 %copy-start.99 = (f32[128]{0:T(128)}, f32[128]{0:T(128)S(1)}, u32[]{:S(2)}) copy-start(f32[128]{0:T(128)S(1)} %get-tuple-element.191) | copy-start | bytes 1540
  146.5 322.0 %copy-start.95 = (f32[128]{0:T(128)}, f32[128]{0:T(128)S(1)}, u32[]{:S(2)}) copy-start(f32[128]{0:T(128)S(1)} %get-tuple-element.206) | copy-start | bytes 1540
  209.3 41.2 %all-to-all-start.4 = ((bf16[64,32,384]{2,1,0:T(8,128)(2,1)}), bf16[64,32,384]{2,1,0:T(8,128)(2,1)}, u32[]{:S(2)}, u32[]{:S(2)}) async-start(bf16[64,32,384]{2,1,0:T(8,128)(2,1)} %copy.496), calls=%async_computation.4 | async-start | bytes 3145728 | tf_op jit(solution)/shard_map/all_to_all | solution.py:46
  250.5 40.8 %all-to-all-start.3 = ((bf16[64,32,384]{2,1,0:T(8,128)(2,1)}), bf16[64,32,384]{2,1,0:T(8,128)(2,1)S(1)}, u32[]{:S(2)}, u32[]{:S(2)}) async-start(bf16[64,32,384]{2,1,0:T(8,128)(2,1)} %copy.488), calls=%async_computation.3 | async-start | bytes 3145728 | tf_op jit(solution)/shard_map/all_to_all | solution.py:46
  291.8 7.7 copy-start.40
  294.6 10.9 %copy-start.42 = (bf16[8,256,64]{2,1,0:T(8,128)(2,1)S(1)}, bf16[8,256,64]{2,1,0:T(8,128)(2,1)}, u32[]{:S(2)}) copy-start(bf16[8,256,64]{2,1,0:T(8,128)(2,1)} %get-tuple-element.135) | copy-start | bytes 786436
  295.6 9.0 %copy-start.43 = (bf16[8,256,64]{2,1,0:T(8,128)(2,1)S(1)}, bf16[8,256,64]{2,1,0:T(8,128)(2,1)}, u32[]{:S(2)}) copy-start(bf16[8,256,64]{2,1,0:T(8,128)(2,1)} %get-tuple-element.134) | copy-start | bytes 786436
  295.6 10.1 %copy-start.88 = (pred[256,256]{0,1:T(8,128)(4,1)S(1)}, pred[256,256]{0,1:T(8,128)(4,1)}, u32[]{:S(2)}) copy-start(pred[256,256]{0,1:T(8,128)(4,1)} %copy-done.87) | copy-start | bytes 196612
  310.6 8.9 %copy-start.11 = (bf16[32,256,128]{1,2,0:T(8,128)(2,1)S(1)}, bf16[32,256,128]{1,2,0:T(8,128)(2,1)}, u32[]{:S(2)}) copy-start(bf16[32,256,128]{1,2,0:T(8,128)(2,1)} %copy-done.10) | copy-start | bytes 6291460
  310.6 41.5 %all-to-all-start.5 = ((bf16[8,256,384]{2,0,1:T(8,128)(2,1)}), bf16[8,256,384]{2,0,1:T(8,128)(2,1)}, u32[]{:S(2)}, u32[]{:S(2)}) async-start(bf16[8,256,384]{2,0,1:T(8,128)(2,1)} %copy.505), calls=%async_computation.5 | async-start | bytes 3145728 | tf_op jit(solution)/shard_map/all_to_all | solution.py:51
  411.1 7.9 copy-start.79
  419.4 8.6 %copy-start.64 = (bf16[8,256,128]{1,2,0:T(8,128)(2,1)S(1)}, bf16[8,256,128]{1,2,0:T(8,128)(2,1)}, u32[]{:S(2)}) copy-start(bf16[8,256,128]{1,2,0:T(8,128)(2,1)} %copy-done.63) | copy-start | bytes 1572868
  423.7 40.5 %all-to-all-start.8 = ((bf16[8,256,384]{2,0,1:T(8,128)(2,1)}), bf16[8,256,384]{2,0,1:T(8,128)(2,1)}, u32[]{:S(2)}, u32[]{:S(2)}) async-start(bf16[8,256,384]{2,0,1:T(8,128)(2,1)} %copy.531), calls=%async_computation.8 | async-start | bytes 3145728 | tf_op jit(solution)/shard_map/all_to_all | solution.py:51
  431.3 37.2 %copy-start.83 = (bf16[1,2,128,128]{3,2,1,0:T(8,128)(2,1)S(1)}, bf16[1,2,128,128]{3,2,1,0:T(8,128)(2,1)}, u32[]{:S(2)}) copy-start(bf16[1,2,128,128]{3,2,1,0:T(8,128)(2,1)} %param.15) | copy-start | bytes 196612
  431.3 37.2 %copy-start.107 = (f32[128]{0:T(128)S(1)}, f32[128]{0:T(128)}, u32[]{:S(2)}) copy-start(f32[128]{0:T(128)} %get-tuple-element.190) | copy-start | bytes 1540
  464.2 40.8 %all-to-all-start.7 = ((bf16[8,256,384]{2,0,1:T(8,128)(2,1)}), bf16[8,256,384]{2,0,1:T(8,128)(2,1)}, u32[]{:S(2)}, u32[]{:S(2)}) async-start(bf16[8,256,384]{2,0,1:T(8,128)(2,1)} %copy.521), calls=%async_computation.7 | async-start | bytes 3145728 | tf_op jit(solution)/shard_map/all_to_all | solution.py:51
  544.7 7.7 copy-start.44
  544.7 7.7 copy-start.45
  574.2 41.2 %all-to-all-start.9 = ((bf16[64,32,384]{2,1,0:T(8,128)(2,1)}), bf16[64,32,384]{2,1,0:T(8,128)(2,1)}, u32[]{:S(2)}, u32[]{:S(2)}) async-start(bf16[64,32,384]{2,1,0:T(8,128)(2,1)} %copy.547), calls=%async_computation.9 | async-start | bytes 3145728 | tf_op jit(solution)/shard_map/all_to_all | solution.py:46
  615.4 14.1 %all-to-all-start.13 = ((bf16[8,16,896]{2,1,0:T(8,128)(2,1)}), bf16[8,16,896]{2,1,0:T(8,128)(2,1)S(1)}, u32[]{:S(2)}, u32[]{:S(2)}) async-start(bf16[8,16,896]{2,1,0:T(8,128)(2,1)} %pad_maximum_fusion.23), calls=%async_computation.13 | async-start | bytes 458752 | tf_op jit(solution)/shard_map/all_to_all | solution.py:63
  627.3 8.2 copy-start.60
  627.3 8.2 copy-start.61
  627.5 8.1 copy-start.69
  629.5 42.7 %all-to-all-start.11 = ((bf16[8,256,384]{2,0,1:T(8,128)(2,1)}), bf16[8,256,384]{2,0,1:T(8,128)(2,1)}, u32[]{:S(2)}, u32[]{:S(2)}) async-start(bf16[8,256,384]{2,0,1:T(8,128)(2,1)} %copy.566), calls=%async_computation.11 | async-start | bytes 3145728 | tf_op jit(solution)/shard_map/all_to_all | solution.py:51
  638.4 38.4 %copy-start.3 = (bf16[1,32,256,128]{2,3,1,0:T(8,128)(2,1)S(1)}, bf16[1,32,256,128]{2,3,1,0:T(8,128)(2,1)}, u32[]{:S(2)}) copy-start(bf16[1,32,256,128]{2,3,1,0:T(8,128)(2,1)} %copy-done.2) | copy-start | bytes 6291460
  638.4 38.4 %copy-start.51 = (f32[32,256]{1,0:T(8,128)S(1)}, f32[32,256]{1,0:T(8,128)}, u32[]{:S(2)}) copy-start(f32[32,256]{1,0:T(8,128)} %copy-done.50) | copy-start | bytes 98308
  638.4 38.4 %copy-start.55 = (f32[32,256]{1,0:T(8,128)S(1)}, f32[32,256]{1,0:T(8,128)}, u32[]{:S(2)}) copy-start(f32[32,256]{1,0:T(8,128)} %copy-done.54) | copy-start | bytes 98308
  638.4 38.4 %copy-start.92 = (f32[128]{0:T(128)S(1)}, f32[128]{0:T(128)}, u32[]{:S(2)}) copy-start(f32[128]{0:T(128)} %copy-done.91) | copy-start | bytes 1540
  638.4 38.4 %copy-start.98 = (f32[128]{0:T(128)S(1)}, f32[128]{0:T(128)}, u32[]{:S(2)}) copy-start(f32[128]{0:T(128)} %copy-done.97) | copy-start | bytes 1540
  672.3 66.9 %all-to-all-start.10 = ((bf16[8,256,384]{2,0,1:T(8,128)(2,1)}), bf16[8,256,384]{2,0,1:T(8,128)(2,1)}, u32[]{:S(2)}, u32[]{:S(2)}) async-start(bf16[8,256,384]{2,0,1:T(8,128)(2,1)} %copy.556), calls=%async_computation.10 | async-start | bytes 3145728 | tf_op jit(solution)/shard_map/all_to_all | solution.py:51
  794.2 47.7 %collective-permute-start = (bf16[32,256,128]{1,2,0:T(8,128)(2,1)S(1)}, bf16[32,256,128]{1,2,0:T(8,128)(2,1)}, u32[]{:S(2)}, u32[]{:S(2)}) collective-permute-start(bf16[32,256,128]{1,2,0:T(8,128)(2,1)S(1)} %fusion.64), channel_id=1, source_target_pairs={{0,24},{8,0},{16,8},{24,16},{1,25},{9,1},{17,9},{25,17},{2,26},{10... | collective-permute-start | bytes 6291464 | tf_op jit(solution)/shard_map/ppermute | solution.py:11
  795.1 12.9 %all-to-all-start.12 = ((bf16[8,16,896]{2,1,0:T(8,128)(2,1)}), bf16[8,16,896]{2,1,0:T(8,128)(2,1)S(1)}, u32[]{:S(2)}, u32[]{:S(2)}) async-start(bf16[8,16,896]{2,1,0:T(8,128)(2,1)} %pad_maximum_fusion.22), calls=%async_computation.12 | async-start | bytes 458752 | tf_op jit(solution)/shard_map/all_to_all | solution.py:63
  (79 other events, 335.7 us)
where the time goes:
time: 857 us; the launch traced here: 846 us
  waiting for transfers between devices  304 us (35%)
  local copies, waits for them, and re-layouts  210 us (25%)
  blocking collectives  116 us (14%)
  other arithmetic  82.6 us (10%)
  matrix products  70 us (8%)
  starting transfers between devices  60.9 us (7%)
    all_to_all x6, waiting for transfers between devices, to_rows(): lax.all_to_all(fold(array), 'row', split_axis=1, concat_axis=0, tiled=True)  149 us
    all_to_all x5, waiting for transfers between devices, to_channels(): lax.all_to_all(fold(array), 'row', split_axis=0, concat_axis=1, tiled=True)  146 us
    unnamed x290, local copies, waits for them, and re-layouts  121 us
    all_gather x2, blocking collectives, reduced(): lax.all_gather(summed, 'row', axis=0, tiled=True).astype(jnp.float32)  74.9 us
    dot_general x24, matrix products, multiply(): jnp.einsum(pattern, first_part, second, preferred_element_type=jnp.float32)  70 us
    all_to_all x1, blocking collectives, to_channels(): lax.all_to_all(fold(array), 'row', split_axis=0, concat_axis=1, tiled=True)  40.7 us
    concatenate x12, local copies, waits for them, and re-layouts, fold(): jnp.concatenate([kept[:half], kept[half:], tail[:half], tail[half:]], axi...  35 us
    all_to_all x6, starting transfers between devices, to_rows(): lax.all_to_all(fold(array), 'row', split_axis=1, concat_axis=0, tiled=True)  28.7 us
  transfers between devices with their start and end apart: 14, of which 11 were waited for; matrix products, arithmetic and copies ran while one was open for 12% of the time, Pallas kernels for 0%

commit v1 on v0

--- a/solution.py
+++ b/solution.py
@@ -48,7 +48,11 @@
 
 
 def to_rows(array, mask):
-    moved = lax.all_to_all(fold(array), "row", split_axis=1, concat_axis=0, tiled=True)
+    block = fold(array)
+    size = lax.axis_size("row")
+    pieces = jnp.stack(jnp.split(block, size, axis=1), axis=0)
+    pieces = lax.all_to_all(pieces, "row", split_axis=0, concat_axis=0)
+    moved = jnp.concatenate(pieces, axis=0)
     return unfold(moved, mask)
 
 

time: 857 us -> 952 us (1.11)
  local copies, waits for them, and re-layouts: 210 us -> 352 us
  waiting for transfers between devices: 304 us -> 258 us
    another operation x0 -> x60, local copies, waits for them, and re-layouts: none -> 99.5 us  [to_rows(): pieces = jnp.stack(jnp.split(block, size, axis=1), axis=0)]
    unnamed x290 -> x362, local copies, waits for them, and re-layouts: 121 us -> 175 us
    all_to_all x6, waiting for transfers between devices: 149 us -> 102 us  [to_rows(): pieces = lax.all_to_all(pieces, 'row', split_axis=0, concat_axis=0)]
    concatenate x12 -> x6, local copies, waits for them, and re-layouts: 35 us -> 19.2 us  [fold(): jnp.concatenate([kept[:half], kept[half:], tail[:half], tail[half:]], axi...]
  transfers between devices with their start and end apart: 14 -> 14, of which waited for: 11 -> 11; matrix products, arithmetic and copies ran while one was open for 12% -> 18% of each run, Pallas kernels for 0% -> 0%
where the time goes in v1:
time: 952 us; the launch traced here: 939 us
  local copies, waits for them, and re-layouts  352 us (37%)
  waiting for transfers between devices  258 us (27%)
  blocking collectives  116 us (12%)
  other arithmetic  77.3 us (8%)
  matrix products  71 us (7%)
  starting transfers between devices  61.3 us (6%)
    unnamed x362, local copies, waits for them, and re-layouts  175 us
    all_to_all x5, waiting for transfers between devices, to_channels(): lax.all_to_all(fold(array), 'row', split_axis=0, concat_axis=1, tiled=True)  147 us
    all_to_all x6, waiting for transfers between devices, to_rows(): pieces = lax.all_to_all(pieces, 'row', split_axis=0, concat_axis=0)  102 us
    another operation x60, local copies, waits for them, and re-layouts, to_rows(): pieces = jnp.stack(jnp.split(block, size, axis=1), axis=0)  99.5 us
    all_gather x2, blocking collectives, reduced(): lax.all_gather(summed, 'row', axis=0, tiled=True).astype(jnp.float32)  74.9 us
    dot_general x24, matrix products, multiply(): jnp.einsum(pattern, first_part, second, preferred_element_type=jnp.float32)  71 us
    all_to_all x1, blocking collectives, to_channels(): lax.all_to_all(fold(array), 'row', split_axis=0, concat_axis=1, tiled=True)  40.8 us
    all_to_all x6, starting transfers between devices, to_rows(): pieces = lax.all_to_all(pieces, 'row', split_axis=0, concat_axis=0)  29 us
  transfers between devices with their start and end apart: 14, of which 11 were waited for; matrix products, arithmetic and copies ran while one was open for 18% of the time, Pallas kernels for 0%

profile of v1, /device:TPU:0, one launch (start us, length us, event | category | flops | bytes accessed | tf_op | source)
XLA Modules:
  0.0 939.2 jit_solution(6094539504073661520)
XLA Ops:
  4.0 3.3 copy.538
  11.6 5.1 multiply_convert_fusion.11
  21.2 4.9 copy.551
  26.1 7.3 all-to-all-start.1
  39.0 4.8 copy.543
  43.8 26.7 %all-to-all-done.1 = bf16[64,32,384]{2,1,0:T(8,128)(2,1)} async-done(((bf16[64,32,384]{2,1,0:T(8,128)(2,1)}), bf16[64,32,384]{2,1,0:T(8,128)(2,1)}, u32[]{:S(2)}, u32[]{:S(2)}) %all-to-all-start.1) | async-done | bytes 1572896 | tf_op jit(solution)/shard_map/all_to_all | solution.py:46
  70.5 4.5 all-to-all-start
  79.4 32.2 %all-to-all-done = bf16[64,32,384]{2,1,0:T(8,128)(2,1)} async-done(((bf16[64,32,384]{2,1,0:T(8,128)(2,1)}), bf16[64,32,384]{2,1,0:T(8,128)(2,1)}, u32[]{:S(2)}, u32[]{:S(2)}) %all-to-all-start) | async-done | bytes 1572896 | tf_op jit(solution)/shard_map/all_to_all | solution.py:46
  137.5 3.9 slice_bitcast_fusion.40
  166.7 4.5 all-to-all-start.2
  171.8 36.0 %all-to-all-done.2 = bf16[8,8,32,384]{3,2,1,0:T(8,128)(2,1)} async-done(((bf16[8,8,32,384]{3,2,1,0:T(8,128)(2,1)}), bf16[8,8,32,384]{3,2,1,0:T(8,128)(2,1)}, u32[]{:S(2)}, u32[]{:S(2)}) %all-to-all-start.2) | async-done | bytes 1572896 | tf_op jit(solution)/shard_map/all_to_all | solution.py:54
  214.9 4.9 convert_reduce_fusion.1
  223.7 5.1 multiply_convert_fusion.9
  235.2 4.8 all-to-all-start.4
  245.1 31.5 %all-to-all-done.4 = bf16[64,32,384]{2,1,0:T(8,128)(2,1)} async-done(((bf16[64,32,384]{2,1,0:T(8,128)(2,1)}), bf16[64,32,384]{2,1,0:T(8,128)(2,1)}, u32[]{:S(2)}, u32[]{:S(2)}) %all-to-all-start.4) | async-done | bytes 1572896 | tf_op jit(solution)/shard_map/all_to_all | solution.py:46
  276.6 3.6 all-to-all-start.3
  283.7 33.7 %all-to-all-done.3 = bf16[64,32,384]{2,1,0:T(8,128)(2,1)S(1)} async-done(((bf16[64,32,384]{2,1,0:T(8,128)(2,1)}), bf16[64,32,384]{2,1,0:T(8,128)(2,1)S(1)}, u32[]{:S(2)}, u32[]{:S(2)}) %all-to-all-start.3) | async-done | bytes 1572896 | tf_op jit(solution)/shard_map/all_to_all | solution.py:46
  353.2 4.6 all-to-all-start.5
  357.8 4.1 copy.537
  362.0 4.5 add_divide_fusion
  366.4 28.0 %all-to-all-done.5 = bf16[8,8,32,384]{3,2,1,0:T(8,128)(2,1)} async-done(((bf16[8,8,32,384]{3,2,1,0:T(8,128)(2,1)}), bf16[8,8,32,384]{3,2,1,0:T(8,128)(2,1)}, u32[]{:S(2)}, u32[]{:S(2)}) %all-to-all-start.5) | async-done | bytes 1572896 | tf_op jit(solution)/shard_map/all_to_all | solution.py:54
  407.5 40.8 %all_to_all.148 = bf16[64,32,384]{2,1,0:T(8,128)(2,1)S(1)} all-to-all(bf16[64,32,384]{2,1,0:T(8,128)(2,1)S(1)} %copy.601), channel_id=1, replica_groups=mesh['section'=4,'row'=8] {'row'}, dimensions={0} | all-to-all | bytes 3145728 | tf_op jit(solution)/shard_map/all_to_all | solution.py:46
  462.5 3.9 slice_bitcast_fusion.16
  491.7 4.4 all-to-all-start.8
  499.6 3.9 slice_bitcast_fusion.24
  528.8 3.6 all-to-all-done.8
  532.4 4.7 all-to-all-start.7
  537.1 6.0 fusion.68
  548.5 24.7 %all-to-all-done.7 = bf16[8,8,32,384]{3,2,1,0:T(8,128)(2,1)} async-done(((bf16[8,8,32,384]{3,2,1,0:T(8,128)(2,1)}), bf16[8,8,32,384]{3,2,1,0:T(8,128)(2,1)}, u32[]{:S(2)}, u32[]{:S(2)}) %all-to-all-start.7) | async-done | bytes 1572896 | tf_op jit(solution)/shard_map/all_to_all | solution.py:54
  607.3 6.6 multiply_convert_fusion.5
  614.0 7.4 multiply_convert_fusion.7
  630.3 4.2 fusion.63
  643.2 4.6 all-to-all-start.9
  655.9 4.8 fusion.98
  661.4 22.8 %all-to-all-done.9 = bf16[64,32,384]{2,1,0:T(8,128)(2,1)} async-done(((bf16[64,32,384]{2,1,0:T(8,128)(2,1)}), bf16[64,32,384]{2,1,0:T(8,128)(2,1)}, u32[]{:S(2)}, u32[]{:S(2)}) %all-to-all-start.9) | async-done | bytes 1572896 | tf_op jit(solution)/shard_map/all_to_all | solution.py:46
  684.3 3.6 all-to-all-start.13
  720.4 6.5 all-to-all-start.11
  753.5 10.0 %all-to-all-done.11 = bf16[8,8,32,384]{3,2,1,0:T(8,128)(2,1)} async-done(((bf16[8,8,32,384]{3,2,1,0:T(8,128)(2,1)}), bf16[8,8,32,384]{3,2,1,0:T(8,128)(2,1)}, u32[]{:S(2)}, u32[]{:S(2)}) %all-to-all-start.11) | async-done | bytes 1572896 | tf_op jit(solution)/shard_map/all_to_all | solution.py:54
  763.5 4.3 all-to-all-start.10
  772.8 3.7 fusion.105
  776.5 4.1 fusion.102
  780.6 44.1 %all_gather.7 = bf16[128,896]{1,0:T(8,128)(2,1)S(1)} all-gather(bf16[16,896]{1,0:T(8,128)(2,1)S(1)} %reduce_sum.265), channel_id=1, replica_groups=mesh['section'=4,'row'=8] {'row'}, dimensions={0}, use_global_device_ids=true | all-gather | bytes 258048 | tf_op jit(solution)/shard_map/all_gather | solution.py:69
  865.5 6.7 multiply_convert_fusion.1
  872.3 5.8 multiply_convert_fusion.3
  888.2 3.8 all-to-all-start.12
  892.0 9.0 all-to-all-done.12
  901.1 30.8 %all_gather.6 = bf16[128,896]{1,0:T(8,128)(2,1)S(1)} all-gather(bf16[16,896]{1,0:T(8,128)(2,1)S(1)} %reduce_sum.260), channel_id=1, replica_groups=mesh['section'=4,'row'=8] {'row'}, dimensions={0}, use_global_device_ids=true | all-gather | bytes 258048 | tf_op jit(solution)/shard_map/all_gather | solution.py:69
  934.9 4.1 copy.702
  (598 shorter events, 398.7 us)
Async XLA Ops:
  7.3 207.5 %copy-start.2 = (bf16[1,32,256,128]{2,3,1,0:T(8,128)(2,1)}, bf16[1,32,256,128]{2,3,1,0:T(8,128)(2,1)S(1)}, u32[]{:S(2)}) copy-start(bf16[1,32,256,128]{2,3,1,0:T(8,128)(2,1)S(1)} %copy.538) | copy-start | bytes 6291460
  7.8 207.0 %copy-start.54 = (f32[32,256]{1,0:T(8,128)}, f32[32,256]{1,0:T(8,128)S(1)}, u32[]{:S(2)}) copy-start(f32[32,256]{1,0:T(8,128)S(1)} %broadcast_multiply_fusion.11) | copy-start | bytes 98308
  8.5 206.3 %copy-start.58 = (f32[32,256]{1,0:T(8,128)}, f32[32,256]{1,0:T(8,128)S(1)}, u32[]{:S(2)}) copy-start(f32[32,256]{1,0:T(8,128)S(1)} %add_rsqrt_fusion.3) | copy-start | bytes 98308
  9.0 205.8 %copy-start.107 = (f32[128]{0:T(128)}, f32[128]{0:T(128)S(1)}, u32[]{:S(2)}) copy-start(f32[128]{0:T(128)S(1)} %get-tuple-element.251) | copy-start | bytes 1540
  9.0 205.8 %copy-start.113 = (f32[128]{0:T(128)}, f32[128]{0:T(128)S(1)}, u32[]{:S(2)}) copy-start(f32[128]{0:T(128)S(1)} %get-tuple-element.245) | copy-start | bytes 1540
  26.1 44.4 %all-to-all-start.1 = ((bf16[64,32,384]{2,1,0:T(8,128)(2,1)}), bf16[64,32,384]{2,1,0:T(8,128)(2,1)}, u32[]{:S(2)}, u32[]{:S(2)}) async-start(bf16[64,32,384]{2,1,0:T(8,128)(2,1)} %copy.551), calls=%async_computation.1 | async-start | bytes 3145728 | tf_op jit(solution)/shard_map/all_to_all | solution.py:46
  70.5 41.1 %all-to-all-start = ((bf16[64,32,384]{2,1,0:T(8,128)(2,1)}), bf16[64,32,384]{2,1,0:T(8,128)(2,1)}, u32[]{:S(2)}, u32[]{:S(2)}) async-start(bf16[64,32,384]{2,1,0:T(8,128)(2,1)} %copy.543), calls=%async_computation | async-start | bytes 3145728 | tf_op jit(solution)/shard_map/all_to_all | solution.py:46
  117.2 9.2 copy-start.40
  119.5 14.7 %copy-start.88 = (bf16[8,256,64]{1,2,0:T(8,128)(2,1)}, bf16[8,256,64]{1,2,0:T(8,128)(2,1)S(1)}, u32[]{:S(2)}) copy-start(bf16[8,256,64]{1,2,0:T(8,128)(2,1)S(1)} %copy.753) | copy-start | bytes 786436
  155.5 15.7 %copy-start.126 = (f32[1,2,128]{2,1,0:T(2,128)S(1)}, f32[1,2,128]{2,1,0:T(2,128)}, u32[]{:S(2)}) copy-start(f32[1,2,128]{2,1,0:T(2,128)} %param.19) | copy-start | bytes 3076
  155.5 15.7 %copy-start.127 = (f32[1,2,128]{2,1,0:T(2,128)S(1)}, f32[1,2,128]{2,1,0:T(2,128)}, u32[]{:S(2)}) copy-start(f32[1,2,128]{2,1,0:T(2,128)} %param.18) | copy-start | bytes 3076
  166.7 41.1 %all-to-all-start.2 = ((bf16[8,8,32,384]{3,2,1,0:T(8,128)(2,1)}), bf16[8,8,32,384]{3,2,1,0:T(8,128)(2,1)}, u32[]{:S(2)}, u32[]{:S(2)}) async-start(bf16[8,8,32,384]{3,2,1,0:T(8,128)(2,1)} %constant_dynamic-update-slice_fusion), calls=%async_computation.2 | async-start | bytes 3145728 | tf_op jit(solution)/shard_map/all_to_all | solution.py:54
  171.7 41.4 %copy-start.109 = (f32[128]{0:T(128)}, f32[128]{0:T(128)S(1)}, u32[]{:S(2)}) copy-start(f32[128]{0:T(128)S(1)} %get-tuple-element.253) | copy-start | bytes 1540
  171.7 41.4 %copy-start.115 = (f32[128]{0:T(128)}, f32[128]{0:T(128)S(1)}, u32[]{:S(2)}) copy-start(f32[128]{0:T(128)S(1)} %get-tuple-element.239) | copy-start | bytes 1540
  171.7 365.3 %copy-start.111 = (f32[128]{0:T(128)}, f32[128]{0:T(128)S(1)}, u32[]{:S(2)}) copy-start(f32[128]{0:T(128)S(1)} %get-tuple-element.254) | copy-start | bytes 1540
  235.2 41.5 %all-to-all-start.4 = ((bf16[64,32,384]{2,1,0:T(8,128)(2,1)}), bf16[64,32,384]{2,1,0:T(8,128)(2,1)}, u32[]{:S(2)}, u32[]{:S(2)}) async-start(bf16[64,32,384]{2,1,0:T(8,128)(2,1)} %copy.580), calls=%async_computation.4 | async-start | bytes 3145728 | tf_op jit(solution)/shard_map/all_to_all | solution.py:46
  276.6 40.8 %all-to-all-start.3 = ((bf16[64,32,384]{2,1,0:T(8,128)(2,1)}), bf16[64,32,384]{2,1,0:T(8,128)(2,1)S(1)}, u32[]{:S(2)}, u32[]{:S(2)}) async-start(bf16[64,32,384]{2,1,0:T(8,128)(2,1)} %copy.572), calls=%async_computation.3 | async-start | bytes 3145728 | tf_op jit(solution)/shard_map/all_to_all | solution.py:46
  353.2 8.7 copy-start.11
  353.2 8.7 copy-start.118
  353.2 41.2 %all-to-all-start.5 = ((bf16[8,8,32,384]{3,2,1,0:T(8,128)(2,1)}), bf16[8,8,32,384]{3,2,1,0:T(8,128)(2,1)}, u32[]{:S(2)}, u32[]{:S(2)}) async-start(bf16[8,8,32,384]{3,2,1,0:T(8,128)(2,1)} %constant_dynamic-update-slice_fusion.8), calls=%async_computation.5 | async-start | bytes 3145728 | tf_op jit(solution)/shard_map/all_to_all | solution.py:54
  399.7 137.4 %copy-start.75 = (f32[32,256]{1,0:T(8,128)}, f32[32,256]{1,0:T(8,128)S(1)}, u32[]{:S(2)}) copy-start(f32[32,256]{1,0:T(8,128)S(1)} %add_rsqrt_fusion) | copy-start | bytes 98308
  450.5 8.8 copy-start.103
  480.5 15.7 %copy-start.83 = (bf16[8,256,128]{1,2,0:T(8,128)(2,1)S(1)}, bf16[8,256,128]{1,2,0:T(8,128)(2,1)}, u32[]{:S(2)}) copy-start(bf16[8,256,128]{1,2,0:T(8,128)(2,1)} %copy-done.82) | copy-start | bytes 1572868
  491.7 40.6 %all-to-all-start.8 = ((bf16[8,8,32,384]{3,2,1,0:T(8,128)(2,1)}), bf16[8,8,32,384]{3,2,1,0:T(8,128)(2,1)}, u32[]{:S(2)}, u32[]{:S(2)}) async-start(bf16[8,8,32,384]{3,2,1,0:T(8,128)(2,1)} %constant_dynamic-update-slice_fusion.24), calls=%async_computation.8 | async-start | bytes 3145728 | tf_op jit(solution)/shard_map/all_to_all | solution.py:54
  517.6 19.5 %copy-start.99 = (bf16[1,2,128,128]{3,2,1,0:T(8,128)(2,1)S(1)}, bf16[1,2,128,128]{3,2,1,0:T(8,128)(2,1)}, u32[]{:S(2)}) copy-start(bf16[1,2,128,128]{3,2,1,0:T(8,128)(2,1)} %param.15) | copy-start | bytes 196612
  517.6 19.6 %copy-start.122 = (f32[128]{0:T(128)S(1)}, f32[128]{0:T(128)}, u32[]{:S(2)}) copy-start(f32[128]{0:T(128)} %get-tuple-element.238) | copy-start | bytes 1540
  532.4 40.9 %all-to-all-start.7 = ((bf16[8,8,32,384]{3,2,1,0:T(8,128)(2,1)}), bf16[8,8,32,384]{3,2,1,0:T(8,128)(2,1)}, u32[]{:S(2)}, u32[]{:S(2)}) async-start(bf16[8,8,32,384]{3,2,1,0:T(8,128)(2,1)} %constant_dynamic-update-slice_fusion.16), calls=%async_computation.7 | async-start | bytes 3145728 | tf_op jit(solution)/shard_map/all_to_all | solution.py:54
  614.0 9.4 %copy-start.72 = (bf16[128,640]{1,0:T(8,128)(2,1)S(1)}, bf16[128,640]{1,0:T(8,128)(2,1)}, u32[]{:S(2)}) copy-start(bf16[128,640]{1,0:T(8,128)(2,1)} %get-tuple-element.232) | copy-start | bytes 491524
  643.2 41.1 %all-to-all-start.9 = ((bf16[64,32,384]{2,1,0:T(8,128)(2,1)}), bf16[64,32,384]{2,1,0:T(8,128)(2,1)}, u32[]{:S(2)}, u32[]{:S(2)}) async-start(bf16[64,32,384]{2,1,0:T(8,128)(2,1)} %copy.647), calls=%async_computation.9 | async-start | bytes 3145728 | tf_op jit(solution)/shard_map/all_to_all | solution.py:46
  684.3 36.1 %all-to-all-start.13 = ((bf16[8,16,896]{2,1,0:T(8,128)(2,1)}), bf16[8,16,896]{2,1,0:T(8,128)(2,1)S(1)}, u32[]{:S(2)}, u32[]{:S(2)}) async-start(bf16[8,16,896]{2,1,0:T(8,128)(2,1)} %pad_maximum_fusion.23), calls=%async_computation.13 | async-start | bytes 458752 | tf_op jit(solution)/shard_map/all_to_all | solution.py:67
  717.7 9.2 copy-start.78
  717.7 9.2 copy-start.89
  717.7 9.2 copy-start.104
  718.0 8.9 copy-start.79
  718.0 8.9 copy-start.90
  720.4 43.1 %all-to-all-start.11 = ((bf16[8,8,32,384]{3,2,1,0:T(8,128)(2,1)}), bf16[8,8,32,384]{3,2,1,0:T(8,128)(2,1)}, u32[]{:S(2)}, u32[]{:S(2)}) async-start(bf16[8,8,32,384]{3,2,1,0:T(8,128)(2,1)} %constant_dynamic-update-slice_fusion.40), calls=%async_computation.11 | async-start | bytes 3145728 | tf_op jit(solution)/shard_map/all_to_all | solution.py:54
  742.2 8.5 copy-start.68
  742.2 9.2 copy-start.66
  742.3 9.9 %copy-start.64 = (bf16[1,8,32,384]{3,2,1,0:T(8,128)(2,1)S(1)}, bf16[1,8,32,384]{3,2,1,0:T(8,128)(2,1)}, u32[]{:S(2)}) copy-start(bf16[1,8,32,384]{3,2,1,0:T(8,128)(2,1)} %copy.662) | copy-start | bytes 589828
  742.3 10.6 %copy-start.62 = (bf16[1,8,32,384]{3,2,1,0:T(8,128)(2,1)S(1)}, bf16[1,8,32,384]{3,2,1,0:T(8,128)(2,1)}, u32[]{:S(2)}) copy-start(bf16[1,8,32,384]{3,2,1,0:T(8,128)(2,1)} %copy.663) | copy-start | bytes 589828
  745.0 22.8 %copy-start.3 = (bf16[1,32,256,128]{2,3,1,0:T(8,128)(2,1)S(1)}, bf16[1,32,256,128]{2,3,1,0:T(8,128)(2,1)}, u32[]{:S(2)}) copy-start(bf16[1,32,256,128]{2,3,1,0:T(8,128)(2,1)} %copy-done.2) | copy-start | bytes 6291460
  745.0 22.8 %copy-start.55 = (f32[32,256]{1,0:T(8,128)S(1)}, f32[32,256]{1,0:T(8,128)}, u32[]{:S(2)}) copy-start(f32[32,256]{1,0:T(8,128)} %copy-done.54) | copy-start | bytes 98308
  745.0 22.8 %copy-start.59 = (f32[32,256]{1,0:T(8,128)S(1)}, f32[32,256]{1,0:T(8,128)}, u32[]{:S(2)}) copy-start(f32[32,256]{1,0:T(8,128)} %copy-done.58) | copy-start | bytes 98308
  745.0 22.8 %copy-start.108 = (f32[128]{0:T(128)S(1)}, f32[128]{0:T(128)}, u32[]{:S(2)}) copy-start(f32[128]{0:T(128)} %copy-done.107) | copy-start | bytes 1540
  745.0 22.8 %copy-start.114 = (f32[128]{0:T(128)S(1)}, f32[128]{0:T(128)}, u32[]{:S(2)}) copy-start(f32[128]{0:T(128)} %copy-done.113) | copy-start | bytes 1540
  763.5 67.7 %all-to-all-start.10 = ((bf16[8,8,32,384]{3,2,1,0:T(8,128)(2,1)}), bf16[8,8,32,384]{3,2,1,0:T(8,128)(2,1)}, u32[]{:S(2)}, u32[]{:S(2)}) async-start(bf16[8,8,32,384]{3,2,1,0:T(8,128)(2,1)} %constant_dynamic-update-slice_fusion.32), calls=%async_computation.10 | async-start | bytes 3145728 | tf_op jit(solution)/shard_map/all_to_all | solution.py:54
  887.2 47.7 %collective-permute-start = (bf16[32,256,128]{1,2,0:T(8,128)(2,1)S(1)}, bf16[32,256,128]{1,2,0:T(8,128)(2,1)}, u32[]{:S(2)}, u32[]{:S(2)}) collective-permute-start(bf16[32,256,128]{1,2,0:T(8,128)(2,1)S(1)} %fusion.64), channel_id=1, source_target_pairs={{0,24},{8,0},{16,8},{24,16},{1,25},{9,1},{17,9},{25,17},{2,26},{10... | collective-permute-start | bytes 6291464 | tf_op jit(solution)/shard_map/ppermute | solution.py:11
  888.2 12.9 %all-to-all-start.12 = ((bf16[8,16,896]{2,1,0:T(8,128)(2,1)}), bf16[8,16,896]{2,1,0:T(8,128)(2,1)S(1)}, u32[]{:S(2)}, u32[]{:S(2)}) async-start(bf16[8,16,896]{2,1,0:T(8,128)(2,1)} %pad_maximum_fusion.22), calls=%async_computation.12 | async-start | bytes 458752 | tf_op jit(solution)/shard_map/all_to_all | solution.py:67
  (94 other events, 393.7 us)
